TPU v7x, 512 devices: a whole 4x8x8 slice. The times are simulated.
512 devices in a mesh: grp: 32 (over x, z), tp: 16 (over y, core).
Axes of the slice: x: 4, y: 8, z: 8, core: 2. Of those that a mesh axis runs over, the one named last changes fastest.
Arguments:
- acts: bfloat16 [4096, 8192], P('grp', 'tp'), may hold values from -6 to 6
- grads: bfloat16 [4096, 4096], P('grp'), may hold values from -1.5 to 1.5
- counts: int32 [32, 24], P('grp'), may hold values from 1 to 12, 128 in all within a row
- owner_slot: int32 [24], replicated, may hold values from 0 to 31, as said below
- base_weight: bfloat16 [8192, 4096], P('tp', 'grp')
- adapter_a: bfloat16 [32, 8192, 32], P('grp', 'tp'), may hold values from -0.0625 to 0.0625
- adapter_b: bfloat16 [32, 32, 4096], P('grp'), may hold values from -0.59765625 to 0.59765625
- magnitude: float32 [32, 4096], P('grp'), may hold values from 0.5 to 2
Outputs:
- row_grad: bfloat16 [4096, 8192], P('grp', 'tp')
- grad_a: float32 [32, 8192, 32], P('grp', 'tp')
- grad_b: float32 [32, 32, 4096], P('grp', None, 'tp')
- grad_gain: float32 [32, 4096], P('grp')
Inputs may be any that keep to these rules, and one draw needn't show every extreme that they name: Every tenant has one row or more on every index of grp; the largest count in each row of counts is exactly 12. `owner_slot`: distinct slots, one for each tenant; slot p lies on index p // 1 of grp; other slots are unused.
All inputs are finite; a program needn't handle non-finite values.
Results may differ from a plain program's by a relative error of at most 0.0095.
Values may be sent and summed in bfloat16 or wider, within the bound.
No kernel may reach another device: no remote copies, remote signals or barrier semaphores. Data moves between devices by JAX's collectives and lax.ppermute only.
A program may use at most 64 MiB of HBM per device.

v0:
```python
import jax
import jax.numpy as jnp
from jax import lax
from jax.sharding import PartitionSpec as P

CAP = 12
NX = 4
EPSILON = 1e-06
HIGH = lax.Precision.HIGHEST
BF = jnp.bfloat16
F32 = jnp.float32


def dot(left, right, dims, precision=None):
    return lax.dot_general(
        left, right, (dims, ((), ())), precision=precision, preferred_element_type=F32
    )


def split_pair(values):
    upper = values.astype(BF)
    return (upper, (values - upper.astype(F32)).astype(BF))


def row_targets(count_row, owner_slot, rows):
    ends = jnp.cumsum(count_row)
    starts = ends - count_row
    ids = jnp.arange(rows, dtype=jnp.int32)[None, :]
    inside = ((ids >= starts[:, None]) & (ids < ends[:, None])).astype(jnp.int32)
    shift = owner_slot * CAP - starts
    return jnp.sum(inside * shift[:, None], axis=0) + ids[0]


def on_device(acts, grads, counts, owner_slot, base_weight, adapter_a, adapter_b, magnitude):
    groups, shards = (lax.axis_size("grp"), lax.axis_size("tp"))
    nz = groups // NX
    quads = shards // NX
    rows, width = acts.shape
    out_width = grads.shape[1]
    rank = adapter_a.shape[2]
    x_cols, t_cols = (out_width // NX, out_width // shards)
    packed = groups * CAP
    z_groups = [[i * nz + j for j in range(nz)] for i in range(NX)]
    x_groups = [[i * nz + j for i in range(NX)] for j in range(nz)]
    my_x = lax.axis_index("grp") // nz
    my_t = lax.axis_index("tp")
    weight_x = lax.all_gather(base_weight.T, "grp", axis=0, tiled=True, axis_index_groups=z_groups)
    target = row_targets(counts[0], owner_slot, rows)
    place = (jnp.arange(packed, dtype=jnp.int32)[:, None] == target[None, :]).astype(BF)
    grads_t = lax.dynamic_slice(grads, (0, my_t * t_cols), (rows, t_cols))
    both = dot(place, jnp.concatenate([acts, grads_t], axis=1), ((1,), (0,))).astype(BF)
    both = lax.all_to_all(
        both.reshape(groups, CAP, width + t_cols), "grp", split_axis=0, concat_axis=0, tiled=True
    ).reshape(packed, width + t_cols)
    rows_in, rows_grad_t = (both[:, :width], both[:, width:])
    rows_grad = lax.all_gather(rows_grad_t, "tp", axis=1, tiled=True)
    first, second = (adapter_a[0], adapter_b[0])
    first_t = first.T
    fields = jnp.concatenate(
        [
            jnp.broadcast_to(first_t[None], (NX, rank, width)),
            second.reshape(rank, NX, x_cols).transpose(1, 0, 2),
        ],
        axis=2,
    )
    fields = lax.all_to_all(
        fields, "grp", split_axis=0, concat_axis=0, tiled=True, axis_index_groups=x_groups
    ).reshape(NX * rank, width + x_cols)
    first_all, second_all = (fields[:, :width], fields[:, width:])
    second_wide = second_all.astype(F32)
    owner = jnp.arange(NX * rank, dtype=jnp.int32) // rank
    gram = jnp.where(owner[:, None] == owner[None, :], dot(first_all, first_all, ((1,), (1,))), 0.0)
    gram_second = dot(gram, second_wide, ((1,), (0,)), HIGH)
    first_weight = dot(first_all, weight_x, ((1,), (1,)))
    square_base = jnp.sum(jnp.square(weight_x.astype(F32)), axis=1)
    squares = square_base[None, :] + jnp.sum(
        (second_wide * (2.0 * first_weight + gram_second)).reshape(NX, rank, x_cols), axis=1
    )
    first_merged = first_weight + gram_second
    rows_low = dot(first_t, rows_in, ((1,), (1,)))

    def lanes(values):
        return jnp.concatenate(
            [values[:, i : i + 128] for i in range(0, values.shape[1], 128)], axis=0
        )

    pieces = first_merged.astype(BF).reshape(NX, rank, quads, t_cols)
    pieces = pieces.transpose(0, 2, 1, 3).reshape(shards, rank, t_cols)
    pieces = jnp.concatenate([pieces[:, :, i : i + 128] for i in range(0, t_cols, 128)], axis=1)
    square_upper, square_lower = split_pair(squares)
    common = jnp.concatenate(
        [lanes(square_upper), lanes(square_lower), lanes(rows_low.astype(BF))], axis=0
    )
    sums = jnp.concatenate(
        [pieces, jnp.broadcast_to(common[None], (shards,) + common.shape)], axis=1
    )
    sums = lax.all_to_all(sums, "tp", split_axis=0, concat_axis=0, tiled=True)
    sums = jnp.sum(sums.astype(F32), axis=0)

    def unlanes(values, height):
        return jnp.concatenate(
            [values[i : i + height] for i in range(0, values.shape[0], height)], axis=1
        )

    n_piece = rank * t_cols // 128
    n_square = NX * x_cols // 128
    merged_piece = unlanes(sums[:n_piece], rank)
    square_sum = unlanes(
        sums[n_piece : n_piece + n_square] + sums[n_piece + n_square : n_piece + 2 * n_square], NX
    )
    rows_low = unlanes(sums[n_piece + 2 * n_square :], rank)
    square_own = lax.all_to_all(
        square_sum.reshape(NX, 1, x_cols),
        "grp",
        split_axis=0,
        concat_axis=0,
        tiled=True,
        axis_index_groups=x_groups,
    ).reshape(1, out_width)
    swap = []
    for i in range(NX):
        for j in range(nz):
            for a in range(NX):
                for q in range(quads):
                    swap.append(
                        (
                            (i * nz + j) * shards + a * quads + q,
                            (a * nz + j) * shards + i * quads + q,
                        )
                    )
    merged_own = lax.ppermute(merged_piece, ("grp", "tp"), swap)
    norm = jnp.sqrt(square_own + EPSILON)
    scale = magnitude / norm

    def along_x(values, step):
        pairs = [((i + step) % NX * nz + j, i * nz + j) for i in range(NX) for j in range(nz)]
        return lax.ppermute(values, "grp", pairs)

    after = along_x(weight_x, 1)
    before = along_x(weight_x, -1)
    half = x_cols // 2
    across = jnp.concatenate([along_x(after[:half], 1), along_x(before[half:], -1)], axis=0)
    weight = jnp.zeros((out_width, width), BF)
    for piece, step in ((weight_x, 0), (after, 1), (across, 2), (before, 3)):
        weight = lax.dynamic_update_slice(weight, piece, ((my_x + step) % NX * x_cols, 0))
    hidden = (rows_grad.astype(F32) * scale).astype(BF)
    inner = dot(hidden, second, ((1,), (1,))).astype(BF)
    back = dot(hidden, weight, ((1,), (0,))) + dot(inner, first, ((1,), (1,)))
    back = lax.all_to_all(
        back.astype(BF).reshape(groups, CAP, width), "grp", split_axis=0, concat_axis=0, tiled=True
    ).reshape(packed, width)
    row_grad = dot(place, back, ((0,), (0,))).astype(BF)
    projected = dot(rows_in, weight, ((1,), (1,)))
    align = jnp.sum(rows_grad.astype(F32) * projected, axis=0)
    second_t = lax.dynamic_slice(second, (0, my_t * t_cols), (rank, t_cols)).astype(F32)
    first_moment = dot(rows_low.astype(BF), rows_grad_t, ((1,), (0,)))
    align_low = jnp.sum(first_moment * second_t, axis=0)
    align_t = lax.dynamic_slice(align, (my_t * t_cols,), (t_cols,)) + align_low
    align = lax.dynamic_update_slice(align, align_t, (my_t * t_cols,))
    align_all = lax.all_to_all(
        jnp.broadcast_to(align.reshape(1, -1, 128), (shards, out_width // 128, 128)),
        "tp",
        split_axis=0,
        concat_axis=0,
        tiled=True,
    )
    align = jnp.sum(align_all, axis=0).reshape(1, out_width)
    grad_gain = align / norm
    shrink = magnitude * align / (norm * norm * norm)
    shrunk = (second.astype(F32) * shrink).astype(BF)
    small = dot(second, shrunk, ((1,), (1,)))
    grad_a = (
        dot(rows_in, inner, ((0,), (0,)))
        - dot(weight, shrunk, ((0,), (1,)))
        - dot(first, small.astype(BF), ((1,), (0,)))
    )
    scale_t = lax.dynamic_slice(scale, (0, my_t * t_cols), (1, t_cols))
    shrink_t = lax.dynamic_slice(shrink, (0, my_t * t_cols), (1, t_cols))
    grad_b = first_moment * scale_t - merged_own * shrink_t
    return (row_grad, grad_a[None], grad_b[None], grad_gain)


def solution(mesh):
    in_specs = (
        P("grp", "tp"),
        P("grp", None),
        P("grp", None),
        P(),
        P("tp", "grp"),
        P("grp", "tp", None),
        P("grp", None, None),
        P("grp", None),
    )
    out_specs = (P("grp", "tp"), P("grp", "tp", None), P("grp", None, "tp"), P("grp", None))
    return jax.shard_map(
        on_device, mesh=mesh, in_specs=in_specs, out_specs=out_specs, check_vma=False
    )
```

profile of v0, /device:TPU:1, one launch (start us, length us, event | category | flops | bytes accessed | tf_op | source)
XLA Modules:
  0.0 199.2 jit_solution(3554385559575562008)
XLA Ops:
  7.2 0.7 all-gather.5.cloned.1.call-update
  7.9 1.1 reshape_squeeze.3
  9.2 0.8 broadcast_in_dim.18
  9.9 0.8 pad_maximum_fusion.1
  10.7 4.8 %all-to-all-start.1 = ((bf16[4,32,1536]{2,1,0:T(8,128)(2,1)}), bf16[4,32,1536]{2,1,0:T(8,128)(2,1)S(1)}, u32[]{:S(2)}, u32[]{:S(2)}) async-start(bf16[4,32,1536]{2,1,0:T(8,128)(2,1)} %pad_maximum_fusion.1), calls=%async_computation.1 | async-start | bytes 786432 | tf_op jit(solution)/shard_map/all_to_all | solution.py:66
  15.5 0.7 copy.21
  16.4 0.7 multiply_subtract_fusion
  17.3 1.2 convolution_convert_fusion
  18.5 1.1 reshape.168
  19.5 2.3 %all-to-all-done.1 = bf16[4,32,1536]{2,1,0:T(8,128)(2,1)S(1)} async-done(((bf16[4,32,1536]{2,1,0:T(8,128)(2,1)}), bf16[4,32,1536]{2,1,0:T(8,128)(2,1)S(1)}, u32[]{:S(2)}, u32[]{:S(2)}) %all-to-all-start.1) | async-done | bytes 393248 | tf_op jit(solution)/shard_map/all_to_all | solution.py:66
  21.8 11.7 %all-to-all-start = ((bf16[32,12,768]{2,1,0:T(8,128)(2,1)}), bf16[32,12,768]{2,1,0:T(8,128)(2,1)S(1)}, u32[]{:S(2)}, u32[]{:S(2)}) async-start(bf16[32,12,768]{2,1,0:T(8,128)(2,1)} %reshape.168), calls=%async_computation | async-start | bytes 1572864 | tf_op jit(solution)/shard_map/all_to_all | solution.py:52
  33.7 26.8 %all-to-all-done = bf16[32,12,768]{2,1,0:T(8,128)(2,1)S(1)} async-done(((bf16[32,12,768]{2,1,0:T(8,128)(2,1)}), bf16[32,12,768]{2,1,0:T(8,128)(2,1)S(1)}, u32[]{:S(2)}, u32[]{:S(2)}) %all-to-all-start) | async-done | bytes 589856 | tf_op jit(solution)/shard_map/all_to_all | solution.py:52
  60.6 0.7 slice.178
  61.7 4.3 %all-gather.5.cloned.1.call-done = bf16[1024,512]{0,1:T(8,128)(2,1)} async-done(((bf16[128,512]{0,1:T(8,128)(2,1)}), bf16[1024,512]{0,1:T(8,128)(2,1)}) %all-gather.5.cloned.1.call-update) | async-done | bytes 1048592 | tf_op jit(solution)/shard_map/all_gather | solution.py:47
  65.9 1.6 fusion.38
  68.9 5.3 %collective-permute-start = (bf16[1024,512]{0,1:T(8,128)(2,1)S(1)}, bf16[1024,512]{0,1:T(8,128)(2,1)}, u32[]{:S(2)}, u32[]{:S(2)}) collective-permute-start(bf16[1024,512]{0,1:T(8,128)(2,1)S(1)} %copy-done.1), channel_id=1, source_target_pairs={{128,0},{144,16},{160,32},{176,48},{192,64},{208,80},{224,96},{240... | collective-permute-start | bytes 3145736 | tf_op jit(solution)/shard_map/ppermute | solution.py:137
  74.2 1.9 collective-permute-start.2
  76.3 1.0 pad_maximum_fusion
  77.3 8.9 %all-to-all-start.2 = ((bf16[16,224,128]{2,1,0:T(8,128)(2,1)}), bf16[16,224,128]{2,1,0:T(8,128)(2,1)S(1)}, u32[]{:S(2)}, u32[]{:S(2)}) async-start(bf16[16,224,128]{2,1,0:T(8,128)(2,1)} %pad_maximum_fusion), calls=%async_computation.2 | async-start | bytes 1835008 | tf_op jit(solution)/shard_map/all_to_all | solution.py:97
  86.2 8.4 %collective-permute-done = bf16[1024,512]{0,1:T(8,128)(2,1)} collective-permute-done((bf16[1024,512]{0,1:T(8,128)(2,1)S(1)}, bf16[1024,512]{0,1:T(8,128)(2,1)}, u32[]{:S(2)}, u32[]{:S(2)}) %collective-permute-start) | collective-permute-done | bytes 1048608 | tf_op jit(solution)/shard_map/ppermute | solution.py:137
  94.6 1.9 slice.213
  96.5 5.4 %collective-permute-start.1 = (bf16[512,512]{0,1:T(8,128)(2,1)}, bf16[512,512]{0,1:T(8,128)(2,1)S(1)}, u32[]{:S(2)}, u32[]{:S(2)}) collective-permute-start(bf16[512,512]{0,1:T(8,128)(2,1)} %slice.213), channel_id=1, source_target_pairs={{128,0},{144,16},{160,32},{176,48},{192,64},{208,80},{224,96},{240... | collective-permute-start | bytes 1572872 | tf_op jit(solution)/shard_map/ppermute | solution.py:137
  101.9 1.9 slice.214
  103.8 1.9 collective-permute-start.3
  105.8 2.5 %broadcast_in_dim.21 = bf16[4096,512]{0,1:T(8,128)(2,1)} broadcast(bf16[]{:T(256)} %constant.83.clone.1), dimensions={} | broadcast | bytes 4194306 | tf_op jit(solution)/shard_map/broadcast_in_dim | solution.py:143
  108.3 1.1 constant_dynamic-update-slice_fusion.10
  109.4 2.4 %constant_dynamic-update-slice_fusion.9 = bf16[4096,512]{0,1:T(8,128)(2,1)} fusion(bf16[4096,512]{0,1:T(8,128)(2,1)} %constant_dynamic-update-slice_fusion.10, bf16[1024,512]{0,1:T(8,128)(2,1)} %collective-permute-done, s32[]{:T(128)S(6)} %select_n.67), kind=kLoop, calls=%fused_computation.87 | loop fusion | bytes 2097156 | tf_op jit(solution)/shard_map/dynamic_update_slice | solution.py:145
  111.8 5.7 %collective-permute-done.3 = bf16[512,512]{0,1:T(8,128)(2,1)} collective-permute-done((bf16[512,512]{0,1:T(8,128)(2,1)}, bf16[512,512]{0,1:T(8,128)(2,1)}, u32[]{:S(2)}, u32[]{:S(2)}) %collective-permute-start.3) | collective-permute-done | bytes 524320 | tf_op jit(solution)/shard_map/ppermute | solution.py:137
  117.4 2.3 %maximum_dynamic-update-slice_fusion = bf16[4096,512]{0,1:T(8,128)(2,1)} fusion(bf16[4096,512]{0,1:T(8,128)(2,1)} %constant_dynamic-update-slice_fusion.9, s32[]{:T(128)S(6)} %select_n.69, bf16[512,512]{0,1:T(8,128)(2,1)} %collective-permute-done.3, bf16[512,512]{0,1:T(8,128)(2,1)S(1)} %collective-permute-done.1), kind=kLoop, calls=%fused_computation.21 | loop fusion | flops 2097152 | bytes 2097156 | tf_op jit(solution)/shard_map/dynamic_update_slice | solution.py:145
  119.7 2.3 %constant_dynamic-update-slice_fusion.8 = bf16[4096,512]{0,1:T(8,128)(2,1)} fusion(bf16[4096,512]{0,1:T(8,128)(2,1)} %maximum_dynamic-update-slice_fusion, bf16[1024,512]{0,1:T(8,128)(2,1)} %collective-permute-done.2, s32[]{:T(128)S(6)} %select_n.71), kind=kLoop, calls=%fused_computation.86 | loop fusion | bytes 2097156 | tf_op jit(solution)/shard_map/dynamic_update_slice | solution.py:145
  122.3 0.6 copy.24
  122.9 3.3 %all-to-all-start.3 = ((f32[4,1,1024]{2,1,0:T(1,128)}), f32[4,1,1024]{2,1,0:T(1,128)S(1)}, u32[]{:S(2)}, u32[]{:S(2)}) async-start(f32[4,1,1024]{2,1,0:T(1,128)} %copy.24), calls=%async_computation.3 | async-start | bytes 32768 | tf_op jit(solution)/shard_map/all_to_all | solution.py:112
  126.4 5.4 %all-gather.3.cloned.1.call-done = bf16[384,4096]{1,0:T(8,128)(2,1)} async-done(((bf16[384,256]{1,0:T(8,128)(2,1)}), bf16[384,4096]{1,0:T(8,128)(2,1)}) %all-gather.3.cloned.1.call-update) | async-done | bytes 3145744 | tf_op jit(solution)/shard_map/all_gather | solution.py:56
  131.7 5.0 %fusion.1 = f32[4096]{0:T(1024)S(1)} fusion(bf16[384,4096]{1,0:T(8,128)(2,1)} %all-gather.3.cloned.1.call-done, bf16[4096,512]{0,1:T(8,128)(2,1)} %constant_dynamic-update-slice_fusion.8, bf16[384,768]{1,0:T(8,128)(2,1)S(1)} %copy-done.4), kind=kOutput, calls=%fused_computation.3 | convolution fusion | flops 1615327232 | bytes 7749632 | tf_op jit(solution)/shard_map/dot_general | solution.py:15
  136.9 0.7 broadcast_in_dim.23
  137.6 4.6 %all-to-all-start.5 = ((f32[16,32,128]{2,1,0:T(8,128)}), f32[16,32,128]{2,1,0:T(8,128)S(1)}, u32[]{:S(2)}, u32[]{:S(2)}) async-start(f32[16,32,128]{2,1,0:T(8,128)} %broadcast_in_dim.23), calls=%async_computation.5 | async-start | bytes 524288 | tf_op jit(solution)/shard_map/all_to_all | solution.py:160
  142.3 0.7 collective-permute-start.4
  143.0 11.0 %all-to-all-done.5 = f32[16,32,128]{2,1,0:T(8,128)S(1)} async-done(((f32[16,32,128]{2,1,0:T(8,128)}), f32[16,32,128]{2,1,0:T(8,128)S(1)}, u32[]{:S(2)}, u32[]{:S(2)}) %all-to-all-start.5) | async-done | bytes 262176 | tf_op jit(solution)/shard_map/all_to_all | solution.py:160
  154.0 0.6 fusion.62
  154.7 3.2 %fusion.14 = bf16[384,32]{0,1:T(8,128)(2,1)S(1)} fusion(bf16[384,4096]{1,0:T(8,128)(2,1)} %all-gather.3.cloned.1.call-done, f32[4096]{0:T(1024)S(1)} %bitcast.82, bf16[1,32,4096]{2,1,0:T(8,128)(2,1)S(1)} %copy-done.2), kind=kOutput, calls=%fused_computation.17 | convolution fusion | flops 105394176 | bytes 3448832 | tf_op jit(solution)/shard_map/dot_general | solution.py:15
  158.4 4.0 %fusion.9 = bf16[384,512]{1,0:T(8,128)(2,1)S(1)} fusion(f32[384,512]{1,0:T(8,128)S(1)} %fusion.43, bf16[4096,512]{0,1:T(8,128)(2,1)} %constant_dynamic-update-slice_fusion.8, bf16[384,4096]{1,0:T(8,128)(2,1)S(1)} %copy-done.8, f32[4096]{0:T(1024)S(1)} %bitcast.83), kind=kOutput, calls=%fused_computation.10 | convolution fusion | flops 1615724544 | bytes 8536064 | tf_op jit(solution)/shard_map/dot_general | solution.py:15
  162.4 0.9 reshape.175
  163.3 11.1 %all-to-all-start.4 = ((bf16[32,12,512]{2,1,0:T(8,128)(2,1)}), bf16[32,12,512]{2,1,0:T(8,128)(2,1)S(1)}, u32[]{:S(2)}, u32[]{:S(2)}) async-start(bf16[32,12,512]{2,1,0:T(8,128)(2,1)} %reshape.175), calls=%async_computation.4 | async-start | bytes 1048576 | tf_op jit(solution)/shard_map/all_to_all | solution.py:149
  174.4 3.5 %convolution_subtract_fusion = f32[512,32]{0,1:T(8,128)S(1)} fusion(f32[512,32]{0,1:T(8,128)S(1)} %fusion.19, bf16[4096,512]{0,1:T(8,128)(2,1)} %constant_dynamic-update-slice_fusion.8, bf16[1,32,4096]{2,1,0:T(8,128)(2,1)S(1)} %copy-done.2, f32[4096]{0:T(1024)S(1)} %bitcast.75), kind=kOutput, calls=%fused_computation.16 | convolution fusion | flops 134627328 | bytes 4603904 | tf_op jit(solution)/shard_map/dot_general | solution.py:15
  178.0 1.0 fusion.13
  178.9 0.6 subtract_bitcast_fusion
  179.6 11.8 %all-to-all-done.4 = bf16[32,12,512]{2,1,0:T(8,128)(2,1)S(1)} async-done(((bf16[32,12,512]{2,1,0:T(8,128)(2,1)}), bf16[32,12,512]{2,1,0:T(8,128)(2,1)S(1)}, u32[]{:S(2)}, u32[]{:S(2)}) %all-to-all-start.4) | async-done | bytes 393248 | tf_op jit(solution)/shard_map/all_to_all | solution.py:149
  191.4 0.9 convolution_convert_fusion.1
  (69 shorter events, 3.7 us)
Async XLA Ops:
  7.2 10.1 %copy-start = (bf16[128,4096]{1,0:T(8,128)(2,1)S(1)}, bf16[128,4096]{1,0:T(8,128)(2,1)}, u32[]{:S(2)}) copy-start(bf16[128,4096]{1,0:T(8,128)(2,1)} %param.9) | copy-start | bytes 3145732
  7.2 58.8 %all-gather.5.cloned.1.call-start = ((), (), s32[]{:S(2)}) async-start(), calls=%async_computation.7 | async-start | bytes 1179648 | tf_op jit(solution)/shard_map/all_gather | solution.py:47
  9.1 52.3 %copy-start.5 = (bf16[1,512,32]{1,2,0:T(8,128)(2,1)S(1)}, bf16[1,512,32]{1,2,0:T(8,128)(2,1)}, u32[]{:S(2)}) copy-start(bf16[1,512,32]{1,2,0:T(8,128)(2,1)} %param.13) | copy-start | bytes 98308
  10.7 11.1 %all-to-all-start.1 = ((bf16[4,32,1536]{2,1,0:T(8,128)(2,1)}), bf16[4,32,1536]{2,1,0:T(8,128)(2,1)S(1)}, u32[]{:S(2)}, u32[]{:S(2)}) async-start(bf16[4,32,1536]{2,1,0:T(8,128)(2,1)} %pad_maximum_fusion.1), calls=%async_computation.1 | async-start | bytes 786432 | tf_op jit(solution)/shard_map/all_to_all | solution.py:66
  21.8 38.7 %all-to-all-start = ((bf16[32,12,768]{2,1,0:T(8,128)(2,1)}), bf16[32,12,768]{2,1,0:T(8,128)(2,1)S(1)}, u32[]{:S(2)}, u32[]{:S(2)}) async-start(bf16[32,12,768]{2,1,0:T(8,128)(2,1)} %reshape.168), calls=%async_computation | async-start | bytes 1572864 | tf_op jit(solution)/shard_map/all_to_all | solution.py:52
  33.5 98.2 %all-gather.3.cloned.1.call-start = ((), (), s32[]{:S(2)}) async-start(), calls=%async_computation.6 | async-start | bytes 3342336 | tf_op jit(solution)/shard_map/all_gather | solution.py:56
  60.6 1.1 copy-start.3
  65.9 2.4 %copy-start.1 = (bf16[1024,512]{0,1:T(8,128)(2,1)S(1)}, bf16[1024,512]{0,1:T(8,128)(2,1)}, u32[]{:S(2)}) copy-start(bf16[1024,512]{0,1:T(8,128)(2,1)} %all-gather.5.cloned.1.call-done) | copy-start | bytes 3145732
  68.9 25.7 %collective-permute-start = (bf16[1024,512]{0,1:T(8,128)(2,1)S(1)}, bf16[1024,512]{0,1:T(8,128)(2,1)}, u32[]{:S(2)}, u32[]{:S(2)}) collective-permute-start(bf16[1024,512]{0,1:T(8,128)(2,1)S(1)} %copy-done.1), channel_id=1, source_target_pairs={{128,0},{144,16},{160,32},{176,48},{192,64},{208,80},{224,96},{240... | collective-permute-start | bytes 3145736 | tf_op jit(solution)/shard_map/ppermute | solution.py:137
  74.2 27.7 %collective-permute-start.2 = (bf16[1024,512]{0,1:T(8,128)(2,1)S(1)}, bf16[1024,512]{0,1:T(8,128)(2,1)}, u32[]{:S(2)}, u32[]{:S(2)}) collective-permute-start(bf16[1024,512]{0,1:T(8,128)(2,1)S(1)} %copy-done.1), channel_id=1, source_target_pairs={{384,0},{400,16},{416,32},{432,48},{448,64},{464,80},{480,96},{496... | collective-permute-start | bytes 3145736 | tf_op jit(solution)/shard_map/ppermute | solution.py:137
  77.3 44.7 %all-to-all-start.2 = ((bf16[16,224,128]{2,1,0:T(8,128)(2,1)}), bf16[16,224,128]{2,1,0:T(8,128)(2,1)S(1)}, u32[]{:S(2)}, u32[]{:S(2)}) async-start(bf16[16,224,128]{2,1,0:T(8,128)(2,1)} %pad_maximum_fusion), calls=%async_computation.2 | async-start | bytes 1835008 | tf_op jit(solution)/shard_map/all_to_all | solution.py:97
  96.5 15.3 %collective-permute-start.1 = (bf16[512,512]{0,1:T(8,128)(2,1)}, bf16[512,512]{0,1:T(8,128)(2,1)S(1)}, u32[]{:S(2)}, u32[]{:S(2)}) collective-permute-start(bf16[512,512]{0,1:T(8,128)(2,1)} %slice.213), channel_id=1, source_target_pairs={{128,0},{144,16},{160,32},{176,48},{192,64},{208,80},{224,96},{240... | collective-permute-start | bytes 1572872 | tf_op jit(solution)/shard_map/ppermute | solution.py:137
  103.8 13.6 %collective-permute-start.3 = (bf16[512,512]{0,1:T(8,128)(2,1)}, bf16[512,512]{0,1:T(8,128)(2,1)}, u32[]{:S(2)}, u32[]{:S(2)}) collective-permute-start(bf16[512,512]{0,1:T(8,128)(2,1)} %slice.214), channel_id=1, source_target_pairs={{384,0},{400,16},{416,32},{432,48},{448,64},{464,80},{480,96},{496... | collective-permute-start | bytes 1572872 | tf_op jit(solution)/shard_map/ppermute | solution.py:137
  109.4 16.8 %copy-start.2 = (bf16[1,32,4096]{2,1,0:T(8,128)(2,1)S(1)}, bf16[1,32,4096]{2,1,0:T(8,128)(2,1)}, u32[]{:S(2)}) copy-start(bf16[1,32,4096]{2,1,0:T(8,128)(2,1)} %param.14) | copy-start | bytes 786436
  109.4 16.8 %copy-start.4 = (bf16[384,768]{1,0:T(8,128)(2,1)S(1)}, bf16[384,768]{1,0:T(8,128)(2,1)}, u32[]{:S(2)}) copy-start(bf16[384,768]{1,0:T(8,128)(2,1)} %copy-done.3) | copy-start | bytes 1769476
  122.9 14.0 %all-to-all-start.3 = ((f32[4,1,1024]{2,1,0:T(1,128)}), f32[4,1,1024]{2,1,0:T(1,128)S(1)}, u32[]{:S(2)}, u32[]{:S(2)}) async-start(f32[4,1,1024]{2,1,0:T(1,128)} %copy.24), calls=%async_computation.3 | async-start | bytes 32768 | tf_op jit(solution)/shard_map/all_to_all | solution.py:112
  126.3 27.7 %copy-start.7 = (f32[1,4096]{1,0:T(1,128)S(1)}, f32[1,4096]{1,0:T(1,128)}, u32[]{:S(2)}) copy-start(f32[1,4096]{1,0:T(1,128)} %param.15) | copy-start | bytes 49156
  136.7 21.3 %copy-start.6 = (bf16[1,512,32]{1,2,0:T(8,128)(2,1)S(1)}, bf16[1,512,32]{1,2,0:T(8,128)(2,1)}, u32[]{:S(2)}) copy-start(bf16[1,512,32]{1,2,0:T(8,128)(2,1)} %param.13) | copy-start | bytes 98308
  137.6 16.3 %all-to-all-start.5 = ((f32[16,32,128]{2,1,0:T(8,128)}), f32[16,32,128]{2,1,0:T(8,128)S(1)}, u32[]{:S(2)}, u32[]{:S(2)}) async-start(f32[16,32,128]{2,1,0:T(8,128)} %broadcast_in_dim.23), calls=%async_computation.5 | async-start | bytes 524288 | tf_op jit(solution)/shard_map/all_to_all | solution.py:160
  142.3 36.7 %collective-permute-start.4 = (f32[32,256]{1,0:T(8,128)S(1)}, f32[32,256]{1,0:T(8,128)S(1)}, u32[]{:S(2)}, u32[]{:S(2)}) collective-permute-start(f32[32,256]{1,0:T(8,128)S(1)} %pad_maximum_fusion.2), channel_id=1, source_target_pairs={{0,0},{1,1},{2,2},{3,3},{4,128},{5,129},{6,130},{7,131},{8,256},{9... | collective-permute-start | bytes 98312 | tf_op jit(solution)/shard_map/ppermute | solution.py:131
  154.0 4.4 %copy-start.8 = (bf16[384,4096]{1,0:T(8,128)(2,1)S(1)}, bf16[384,4096]{1,0:T(8,128)(2,1)}, u32[]{:S(2)}) copy-start(bf16[384,4096]{1,0:T(8,128)(2,1)} %all-gather.3.cloned.1.call-done) | copy-start | bytes 9437188
  163.3 28.0 %all-to-all-start.4 = ((bf16[32,12,512]{2,1,0:T(8,128)(2,1)}), bf16[32,12,512]{2,1,0:T(8,128)(2,1)S(1)}, u32[]{:S(2)}, u32[]{:S(2)}) async-start(bf16[32,12,512]{2,1,0:T(8,128)(2,1)} %reshape.175), calls=%async_computation.4 | async-start | bytes 1048576 | tf_op jit(solution)/shard_map/all_to_all | solution.py:149
Sparse Core Ops, SparseCore 0:
  10.0 55.8 all-gather.4
  68.0 63.6 all-gather.2
where the time goes:
time: 200 us; the launch traced here: 199 us
  waiting for transfers between devices  76.2 us (38%)
  starting transfers between devices  59.7 us (30%)
  matrix products  22 us (11%)
  local copies, waits for them, and re-layouts  19.8 us (10%)
  between operations  14.6 us (7%)
  other arithmetic  6.93 us (3%)
    all_to_all x1, waiting for transfers between devices, on_device(): lax.all_to_all(both.reshape(groups, CAP, width + t_cols), 'grp', split_ax...  26.8 us
    dot_general x14, matrix products, dot(): lax.dot_general(left, right, (dims, ((), ())), precision=precision, prefe...  22 us
    ppermute x4, starting transfers between devices, along_x(): return lax.ppermute(values, 'grp', pairs)  14.5 us
    ppermute x4, waiting for transfers between devices, along_x(): return lax.ppermute(values, 'grp', pairs)  14.1 us
    all_to_all x1, waiting for transfers between devices, on_device(): lax.all_to_all(back.astype(BF).reshape(groups, CAP, width), 'grp', split_...  11.8 us
    all_to_all x1, starting transfers between devices, on_device(): lax.all_to_all(both.reshape(groups, CAP, width + t_cols), 'grp', split_ax...  11.7 us
    all_to_all x1, starting transfers between devices, on_device(): lax.all_to_all(back.astype(BF).reshape(groups, CAP, width), 'grp', split_...  11.1 us
    all_to_all x1, waiting for transfers between devices, on_device(): lax.all_to_all(jnp.broadcast_to(align.reshape(1, -1, 128), (shards, out_w...  11 us
  transfers between devices with their start and end apart: 13, of which 8 were waited for; matrix products, arithmetic and copies ran while one was open for 24% of the time, Pallas kernels for 0%

commit v1 on v0

--- a/solution.py
+++ b/solution.py
@@ -53,7 +53,12 @@
         both.reshape(groups, CAP, width + t_cols), "grp", split_axis=0, concat_axis=0, tiled=True
     ).reshape(packed, width + t_cols)
     rows_in, rows_grad_t = (both[:, :width], both[:, width:])
-    rows_grad = lax.all_gather(rows_grad_t, "tp", axis=1, tiled=True)
+    rows_grad = jnp.concatenate(
+        jax.lax.all_to_all(
+            jnp.stack([rows_grad_t for _ in range(jax.lax.axis_size("tp"))]), "tp", 0, 0
+        ),
+        axis=1,
+    )
     first, second = (adapter_a[0], adapter_b[0])
     first_t = first.T
     fields = jnp.concatenate(

time: 200 us -> 276 us (1.38)
  waiting for transfers between devices: 76.2 us -> 125 us
  other arithmetic: 6.93 us -> 19.7 us
  local copies, waits for them, and re-layouts: 19.8 us -> 30.2 us
  starting transfers between devices: 59.7 us -> 63.5 us
    all_to_all x1, waiting for transfers between devices: 0.01 us -> 25.4 us  [on_device(): sums = lax.all_to_all(sums, 'tp', split_axis=0, concat_axis=0, tiled=True)]
    all_to_all x0 -> x1, waiting for transfers between devices: none -> 16.3 us  [on_device(): jax.lax.all_to_all(jnp.stack([rows_grad_t for _ in range(jax.lax.axis_siz...]
    ppermute x4, waiting for transfers between devices: 14.1 us -> 28.1 us  [along_x(): return lax.ppermute(values, 'grp', pairs)]
    convert_element_type x0 -> x2, other arithmetic: none -> 7.56 us  [on_device(): hidden = (rows_grad.astype(F32) * scale).astype(BF)]
    convert_element_type x0 -> x1, local copies, waits for them, and re-layouts: none -> 6.56 us  [on_device(): hidden = (rows_grad.astype(F32) * scale).astype(BF)]
    all_gather x1 -> x0, waiting for transfers between devices: 5.35 us -> none  [on_device(): rows_grad = lax.all_gather(rows_grad_t, 'tp', axis=1, tiled=True)]
    all_to_all x0 -> x1, local copies, waits for them, and re-layouts: none -> 4.65 us  [on_device(): jax.lax.all_to_all(jnp.stack([rows_grad_t for _ in range(jax.lax.axis_siz...]
    all_to_all x0 -> x1, starting transfers between devices: none -> 4.37 us  [on_device(): jax.lax.all_to_all(jnp.stack([rows_grad_t for _ in range(jax.lax.axis_siz...]
  transfers between devices with their start and end apart: 13 -> 13, of which waited for: 8 -> 10; matrix products, arithmetic and copies ran while one was open for 24% -> 23% of each run, Pallas kernels for 0% -> 0%
where the time goes in v1:
time: 276 us; the launch traced here: 274 us
  waiting for transfers between devices  125 us (45%)
  starting transfers between devices  63.5 us (23%)
  local copies, waits for them, and re-layouts  30.2 us (11%)
  matrix products  21 us (8%)
  other arithmetic  19.7 us (7%)
  between operations  14.6 us (5%)
    ppermute x4, waiting for transfers between devices, along_x(): return lax.ppermute(values, 'grp', pairs)  28.1 us
    all_to_all x1, waiting for transfers between devices, on_device(): lax.all_to_all(both.reshape(groups, CAP, width + t_cols), 'grp', split_ax...  26.6 us
    all_to_all x1, waiting for transfers between devices, on_device(): sums = lax.all_to_all(sums, 'tp', split_axis=0, concat_axis=0, tiled=True)  25.4 us
    dot_general x14, matrix products, dot(): lax.dot_general(left, right, (dims, ((), ())), precision=precision, prefe...  21 us
    all_to_all x1, waiting for transfers between devices, on_device(): jax.lax.all_to_all(jnp.stack([rows_grad_t for _ in range(jax.lax.axis_siz...  16.3 us
    ppermute x4, starting transfers between devices, along_x(): return lax.ppermute(values, 'grp', pairs)  13 us
    all_to_all x1, starting transfers between devices, on_device(): lax.all_to_all(both.reshape(groups, CAP, width + t_cols), 'grp', split_ax...  11.7 us
    all_to_all x1, waiting for transfers between devices, on_device(): lax.all_to_all(back.astype(BF).reshape(groups, CAP, width), 'grp', split_...  11.2 us
  transfers between devices with their start and end apart: 13, of which 10 were waited for; matrix products, arithmetic and copies ran while one was open for 23% of the time, Pallas kernels for 0%

profile of v1, /device:TPU:1, one launch (start us, length us, event | category | flops | bytes accessed | tf_op | source)
XLA Modules:
  0.0 274.3 jit_solution(12453741718198058249)
XLA Ops:
  7.9 1.1 reshape_squeeze.3
  10.7 4.8 %all-to-all-start.2 = ((bf16[4,32,1536]{2,1,0:T(8,128)(2,1)}), bf16[4,32,1536]{2,1,0:T(8,128)(2,1)S(1)}, u32[]{:S(2)}, u32[]{:S(2)}) async-start(bf16[4,32,1536]{2,1,0:T(8,128)(2,1)} %pad_maximum_fusion.1), calls=%async_computation.2 | async-start | bytes 786432 | tf_op jit(solution)/shard_map/all_to_all | solution.py:71
  17.3 1.2 convolution_convert_fusion
  18.5 1.0 reshape.180
  19.5 2.3 all-to-all-done.2
  21.8 11.7 %all-to-all-start = ((bf16[32,12,768]{2,1,0:T(8,128)(2,1)}), bf16[32,12,768]{2,1,0:T(8,128)(2,1)S(1)}, u32[]{:S(2)}, u32[]{:S(2)}) async-start(bf16[32,12,768]{2,1,0:T(8,128)(2,1)} %reshape.180), calls=%async_computation | async-start | bytes 1572864 | tf_op jit(solution)/shard_map/all_to_all | solution.py:52
  33.7 26.6 %all-to-all-done = bf16[32,12,768]{2,1,0:T(8,128)(2,1)S(1)} async-done(((bf16[32,12,768]{2,1,0:T(8,128)(2,1)}), bf16[32,12,768]{2,1,0:T(8,128)(2,1)S(1)}, u32[]{:S(2)}, u32[]{:S(2)}) %all-to-all-start) | async-done | bytes 589856 | tf_op jit(solution)/shard_map/all_to_all | solution.py:52
  60.7 5.6 %all-gather.2.cloned.1.call-done = bf16[1024,512]{0,1:T(8,128)(2,1)} async-done(((bf16[128,512]{0,1:T(8,128)(2,1)}), bf16[1024,512]{0,1:T(8,128)(2,1)}) %all-gather.2.cloned.1.call-update) | async-done | bytes 1048592 | tf_op jit(solution)/shard_map/all_gather | solution.py:47
  66.4 1.6 fusion.27
  69.5 1.0 pad_maximum_fusion
  70.5 9.2 %all-to-all-start.3 = ((bf16[16,224,128]{2,1,0:T(8,128)(2,1)}), bf16[16,224,128]{2,1,0:T(8,128)(2,1)}, u32[]{:S(2)}, u32[]{:S(2)}) async-start(bf16[16,224,128]{2,1,0:T(8,128)(2,1)} %pad_maximum_fusion), calls=%async_computation.3 | async-start | bytes 1835008 | tf_op jit(solution)/shard_map/all_to_all | solution.py:102
  79.7 25.4 %all-to-all-done.3 = bf16[16,224,128]{2,1,0:T(8,128)(2,1)} async-done(((bf16[16,224,128]{2,1,0:T(8,128)(2,1)}), bf16[16,224,128]{2,1,0:T(8,128)(2,1)}, u32[]{:S(2)}, u32[]{:S(2)}) %all-to-all-start.3) | async-done | bytes 917536 | tf_op jit(solution)/shard_map/all_to_all | solution.py:102
  105.1 2.0 stack.2
  107.1 4.4 %all-to-all-start.1 = ((bf16[16,384,256]{2,1,0:T(8,128)(2,1)}), bf16[16,384,256]{2,1,0:T(8,128)(2,1)}, u32[]{:S(2)}, u32[]{:S(2)}) async-start(bf16[16,384,256]{2,1,0:T(8,128)(2,1)} %stack.2), calls=%async_computation.1 | async-start | bytes 6291456 | tf_op jit(solution)/shard_map/all_to_all | solution.py:57
  111.5 3.1 %collective-permute-start.2 = (bf16[1024,512]{0,1:T(8,128)(2,1)S(1)}, bf16[1024,512]{0,1:T(8,128)(2,1)S(1)}, u32[]{:S(2)}, u32[]{:S(2)}) collective-permute-start(bf16[1024,512]{0,1:T(8,128)(2,1)S(1)} %copy-done.1), channel_id=1, source_target_pairs={{384,0},{400,16},{416,32},{432,48},{448,64},{464,80},{480,96},{496... | collective-permute-start | bytes 3145736 | tf_op jit(solution)/shard_map/ppermute | solution.py:142
  114.6 3.4 %collective-permute-start = (bf16[1024,512]{0,1:T(8,128)(2,1)S(1)}, bf16[1024,512]{0,1:T(8,128)(2,1)S(1)}, u32[]{:S(2)}, u32[]{:S(2)}) collective-permute-start(bf16[1024,512]{0,1:T(8,128)(2,1)S(1)} %copy-done.1), channel_id=1, source_target_pairs={{128,0},{144,16},{160,32},{176,48},{192,64},{208,80},{224,96},{240... | collective-permute-start | bytes 3145736 | tf_op jit(solution)/shard_map/ppermute | solution.py:142
  118.0 21.5 %collective-permute-done.2 = bf16[1024,512]{0,1:T(8,128)(2,1)S(1)} collective-permute-done((bf16[1024,512]{0,1:T(8,128)(2,1)S(1)}, bf16[1024,512]{0,1:T(8,128)(2,1)S(1)}, u32[]{:S(2)}, u32[]{:S(2)}) %collective-permute-start.2) | collective-permute-done | bytes 1048608 | tf_op jit(solution)/shard_map/ppermute | solution.py:142
  140.3 1.9 collective-permute-start.3
  142.3 0.9 slice.213
  143.5 4.6 %collective-permute-start.1 = (bf16[512,512]{0,1:T(8,128)(2,1)}, bf16[512,512]{0,1:T(8,128)(2,1)}, u32[]{:S(2)}, u32[]{:S(2)}) collective-permute-start(bf16[512,512]{0,1:T(8,128)(2,1)} %slice.213), channel_id=1, source_target_pairs={{128,0},{144,16},{160,32},{176,48},{192,64},{208,80},{224,96},{240... | collective-permute-start | bytes 1572872 | tf_op jit(solution)/shard_map/ppermute | solution.py:142
  148.2 2.5 broadcast_in_dim.21
  150.6 1.1 constant_dynamic-update-slice_fusion.10
  151.7 1.1 constant_dynamic-update-slice_fusion.9
  152.8 4.6 %collective-permute-done.3 = bf16[512,512]{0,1:T(8,128)(2,1)} collective-permute-done((bf16[512,512]{0,1:T(8,128)(2,1)}, bf16[512,512]{0,1:T(8,128)(2,1)}, u32[]{:S(2)}, u32[]{:S(2)}) %collective-permute-start.3) | collective-permute-done | bytes 524320 | tf_op jit(solution)/shard_map/ppermute | solution.py:142
  157.3 2.1 collective-permute-done.1
  159.4 2.4 maximum_dynamic-update-slice_fusion
  161.8 1.1 constant_dynamic-update-slice_fusion.8
  163.0 1.3 convert_reduce_fusion
  165.2 16.3 %all-to-all-done.1 = bf16[16,384,256]{2,1,0:T(8,128)(2,1)} async-done(((bf16[16,384,256]{2,1,0:T(8,128)(2,1)}), bf16[16,384,256]{2,1,0:T(8,128)(2,1)}, u32[]{:S(2)}, u32[]{:S(2)}) %all-to-all-start.1) | async-done | bytes 3145760 | tf_op jit(solution)/shard_map/all_to_all | solution.py:57
  181.5 4.0 %all-to-all-start.4 = ((f32[4,1,1024]{2,1,0:T(1,128)}), f32[4,1,1024]{2,1,0:T(1,128)S(1)}, u32[]{:S(2)}, u32[]{:S(2)}) async-start(f32[4,1,1024]{2,1,0:T(1,128)} %copy.33), calls=%async_computation.4 | async-start | bytes 32768 | tf_op jit(solution)/shard_map/all_to_all | solution.py:117
  185.5 4.6 %copy.29 = bf16[16,384,256]{1,2,0:T(8,128)(2,1)} copy(bf16[16,384,256]{2,1,0:T(8,128)(2,1)} %all-to-all-done.1) | data formatting | bytes 6291456 | tf_op jit(solution)/shard_map/all_to_all | solution.py:57
  190.1 5.2 %convert_element_type.122 = f32[16,384,256]{1,2,0:T(8,128)} convert(bf16[16,384,256]{1,2,0:T(8,128)(2,1)} %copy.29) | non-fusion elementwise | flops 1572864 | bytes 9437184 | tf_op jit(solution)/shard_map/convert_element_type | solution.py:151
  195.3 6.6 %copy.34 = f32[384,4096]{1,0:T(8,128)} copy(f32[384,4096]{0,1:T(8,128)} %bitcast.76) | data formatting | bytes 12582912 | tf_op jit(solution)/shard_map/convert_element_type | solution.py:151
  201.8 5.9 %multiply_reduce_fusion = f32[4096]{0:T(1024)S(1)} fusion(f32[384,4096]{1,0:T(8,128)} %copy.34, bf16[4096,512]{0,1:T(8,128)(2,1)} %constant_dynamic-update-slice_fusion.8, bf16[384,768]{1,0:T(8,128)(2,1)S(1)} %reshape.181), kind=kOutput, calls=%fused_computation | convolution fusion | flops 1613754368 | bytes 10895360 | tf_op jit(solution)/shard_map/dot_general | solution.py:15
  208.6 5.7 %all-to-all-start.6 = ((f32[16,32,128]{2,1,0:T(8,128)}), f32[16,32,128]{2,1,0:T(8,128)}, u32[]{:S(2)}, u32[]{:S(2)}) async-start(f32[16,32,128]{2,1,0:T(8,128)} %broadcast_in_dim.23), calls=%async_computation.6 | async-start | bytes 524288 | tf_op jit(solution)/shard_map/all_to_all | solution.py:165
  215.0 2.0 collective-permute-start.4
  217.0 9.1 %all-to-all-done.6 = f32[16,32,128]{2,1,0:T(8,128)} async-done(((f32[16,32,128]{2,1,0:T(8,128)}), f32[16,32,128]{2,1,0:T(8,128)}, u32[]{:S(2)}, u32[]{:S(2)}) %all-to-all-start.6) | async-done | bytes 262176 | tf_op jit(solution)/shard_map/all_to_all | solution.py:165
  226.2 1.1 reduce_sum.69
  227.8 2.0 fusion.47
  229.9 2.4 multiply_convert_fusion
  233.9 4.8 %fusion.3 = bf16[384,512]{1,0:T(8,128)(2,1)} fusion(f32[384,512]{1,0:T(8,128)S(1)} %fusion.32, bf16[4096,512]{0,1:T(8,128)(2,1)} %constant_dynamic-update-slice_fusion.8, f32[384,4096]{1,0:T(8,128)S(1)} %bitcast.78, f32[4096]{0:T(1024)S(1)} %bitcast.94), kind=kOutput, calls=%fused_computation.9 | convolution fusion | flops 1614151680 | bytes 11681792 | tf_op jit(solution)/shard_map/dot_general | solution.py:15
  238.7 1.9 reshape.187
  240.6 8.7 %all-to-all-start.5 = ((bf16[32,12,512]{2,1,0:T(8,128)(2,1)}), bf16[32,12,512]{2,1,0:T(8,128)(2,1)S(1)}, u32[]{:S(2)}, u32[]{:S(2)}) async-start(bf16[32,12,512]{2,1,0:T(8,128)(2,1)} %reshape.187), calls=%async_computation.5 | async-start | bytes 1048576 | tf_op jit(solution)/shard_map/all_to_all | solution.py:154
  249.3 3.5 %convolution_subtract_fusion = f32[512,32]{0,1:T(8,128)S(1)} fusion(f32[512,32]{0,1:T(8,128)S(1)} %fusion.8, bf16[4096,512]{0,1:T(8,128)(2,1)} %constant_dynamic-update-slice_fusion.8, bf16[1,32,4096]{2,1,0:T(8,128)(2,1)S(1)} %copy-done.2, f32[4096]{0:T(1024)S(1)} %bitcast.86), kind=kOutput, calls=%fused_computation.15 | convolution fusion | flops 134627328 | bytes 4603904 | tf_op jit(solution)/shard_map/dot_general | solution.py:15
  252.8 1.0 fusion.5
  253.8 1.4 subtract_bitcast_fusion
  255.2 11.2 %all-to-all-done.5 = bf16[32,12,512]{2,1,0:T(8,128)(2,1)S(1)} async-done(((bf16[32,12,512]{2,1,0:T(8,128)(2,1)}), bf16[32,12,512]{2,1,0:T(8,128)(2,1)S(1)}, u32[]{:S(2)}, u32[]{:S(2)}) %all-to-all-start.5) | async-done | bytes 393248 | tf_op jit(solution)/shard_map/all_to_all | solution.py:154
  266.5 0.9 convolution_convert_fusion.1
  (90 shorter events, 12.0 us)
Async XLA Ops:
  7.2 10.1 %copy-start = (bf16[128,4096]{1,0:T(8,128)(2,1)S(1)}, bf16[128,4096]{1,0:T(8,128)(2,1)}, u32[]{:S(2)}) copy-start(bf16[128,4096]{1,0:T(8,128)(2,1)} %param.9) | copy-start | bytes 3145732
  7.2 59.2 %all-gather.2.cloned.1.call-start = ((), (), s32[]{:S(2)}) async-start(), calls=%async_computation.7 | async-start | bytes 1179648 | tf_op jit(solution)/shard_map/all_gather | solution.py:47
  7.9 52.5 %copy-start.9 = (bf16[1,512,32]{1,2,0:T(8,128)(2,1)S(1)}, bf16[1,512,32]{1,2,0:T(8,128)(2,1)}, u32[]{:S(2)}) copy-start(bf16[1,512,32]{1,2,0:T(8,128)(2,1)} %param.13) | copy-start | bytes 98308
  10.7 11.1 %all-to-all-start.2 = ((bf16[4,32,1536]{2,1,0:T(8,128)(2,1)}), bf16[4,32,1536]{2,1,0:T(8,128)(2,1)S(1)}, u32[]{:S(2)}, u32[]{:S(2)}) async-start(bf16[4,32,1536]{2,1,0:T(8,128)(2,1)} %pad_maximum_fusion.1), calls=%async_computation.2 | async-start | bytes 786432 | tf_op jit(solution)/shard_map/all_to_all | solution.py:71
  17.2 43.1 %copy-start.12 = (s32[128]{0:T(128)}, s32[128]{0:T(128)S(1)}, u32[]{:S(2)}) copy-start(s32[128]{0:T(128)S(1)} %iota_add_fusion) | copy-start | bytes 1540
  21.8 38.5 %all-to-all-start = ((bf16[32,12,768]{2,1,0:T(8,128)(2,1)}), bf16[32,12,768]{2,1,0:T(8,128)(2,1)S(1)}, u32[]{:S(2)}, u32[]{:S(2)}) async-start(bf16[32,12,768]{2,1,0:T(8,128)(2,1)} %reshape.180), calls=%async_computation | async-start | bytes 1572864 | tf_op jit(solution)/shard_map/all_to_all | solution.py:52
  60.4 141.4 %copy-start.3 = (bf16[384,768]{1,0:T(8,128)(2,1)}, bf16[384,768]{1,0:T(8,128)(2,1)S(1)}, u32[]{:S(2)}) copy-start(bf16[384,768]{1,0:T(8,128)(2,1)S(1)} %reshape.181) | copy-start | bytes 1769476
  66.4 2.5 copy-start.1
  70.5 34.6 %all-to-all-start.3 = ((bf16[16,224,128]{2,1,0:T(8,128)(2,1)}), bf16[16,224,128]{2,1,0:T(8,128)(2,1)}, u32[]{:S(2)}, u32[]{:S(2)}) async-start(bf16[16,224,128]{2,1,0:T(8,128)(2,1)} %pad_maximum_fusion), calls=%async_computation.3 | async-start | bytes 1835008 | tf_op jit(solution)/shard_map/all_to_all | solution.py:102
  107.1 74.4 %all-to-all-start.1 = ((bf16[16,384,256]{2,1,0:T(8,128)(2,1)}), bf16[16,384,256]{2,1,0:T(8,128)(2,1)}, u32[]{:S(2)}, u32[]{:S(2)}) async-start(bf16[16,384,256]{2,1,0:T(8,128)(2,1)} %stack.2), calls=%async_computation.1 | async-start | bytes 6291456 | tf_op jit(solution)/shard_map/all_to_all | solution.py:57
  111.5 28.0 %collective-permute-start.2 = (bf16[1024,512]{0,1:T(8,128)(2,1)S(1)}, bf16[1024,512]{0,1:T(8,128)(2,1)S(1)}, u32[]{:S(2)}, u32[]{:S(2)}) collective-permute-start(bf16[1024,512]{0,1:T(8,128)(2,1)S(1)} %copy-done.1), channel_id=1, source_target_pairs={{384,0},{400,16},{416,32},{432,48},{448,64},{464,80},{480,96},{496... | collective-permute-start | bytes 3145736 | tf_op jit(solution)/shard_map/ppermute | solution.py:142
  114.6 27.6 %collective-permute-start = (bf16[1024,512]{0,1:T(8,128)(2,1)S(1)}, bf16[1024,512]{0,1:T(8,128)(2,1)S(1)}, u32[]{:S(2)}, u32[]{:S(2)}) collective-permute-start(bf16[1024,512]{0,1:T(8,128)(2,1)S(1)} %copy-done.1), channel_id=1, source_target_pairs={{128,0},{144,16},{160,32},{176,48},{192,64},{208,80},{224,96},{240... | collective-permute-start | bytes 3145736 | tf_op jit(solution)/shard_map/ppermute | solution.py:142
  139.4 2.8 %copy-start.5 = (bf16[1024,512]{0,1:T(8,128)(2,1)}, bf16[1024,512]{0,1:T(8,128)(2,1)S(1)}, u32[]{:S(2)}) copy-start(bf16[1024,512]{0,1:T(8,128)(2,1)S(1)} %collective-permute-done.2) | copy-start | bytes 3145732
  140.3 17.0 %collective-permute-start.3 = (bf16[512,512]{0,1:T(8,128)(2,1)}, bf16[512,512]{0,1:T(8,128)(2,1)}, u32[]{:S(2)}, u32[]{:S(2)}) collective-permute-start(bf16[512,512]{0,1:T(8,128)(2,1)} %slice.214), channel_id=1, source_target_pairs={{384,0},{400,16},{416,32},{432,48},{448,64},{464,80},{480,96},{496... | collective-permute-start | bytes 1572872 | tf_op jit(solution)/shard_map/ppermute | solution.py:142
  142.2 1.2 copy-start.7
  143.5 16.0 %collective-permute-start.1 = (bf16[512,512]{0,1:T(8,128)(2,1)}, bf16[512,512]{0,1:T(8,128)(2,1)}, u32[]{:S(2)}, u32[]{:S(2)}) collective-permute-start(bf16[512,512]{0,1:T(8,128)(2,1)} %slice.213), channel_id=1, source_target_pairs={{128,0},{144,16},{160,32},{176,48},{192,64},{208,80},{224,96},{240... | collective-permute-start | bytes 1572872 | tf_op jit(solution)/shard_map/ppermute | solution.py:142
  148.1 3.5 %copy-start.8 = (bf16[1024,512]{0,1:T(8,128)(2,1)S(1)}, bf16[1024,512]{0,1:T(8,128)(2,1)}, u32[]{:S(2)}) copy-start(bf16[1024,512]{0,1:T(8,128)(2,1)} %copy-done.7) | copy-start | bytes 3145732
  150.6 11.2 %copy-start.6 = (bf16[1024,512]{0,1:T(8,128)(2,1)S(1)}, bf16[1024,512]{0,1:T(8,128)(2,1)}, u32[]{:S(2)}) copy-start(bf16[1024,512]{0,1:T(8,128)(2,1)} %copy-done.5) | copy-start | bytes 3145732
  151.7 13.3 %copy-start.2 = (bf16[1,32,4096]{2,1,0:T(8,128)(2,1)S(1)}, bf16[1,32,4096]{2,1,0:T(8,128)(2,1)}, u32[]{:S(2)}) copy-start(bf16[1,32,4096]{2,1,0:T(8,128)(2,1)} %param.14) | copy-start | bytes 786436
  181.5 26.4 %all-to-all-start.4 = ((f32[4,1,1024]{2,1,0:T(1,128)}), f32[4,1,1024]{2,1,0:T(1,128)S(1)}, u32[]{:S(2)}, u32[]{:S(2)}) async-start(f32[4,1,1024]{2,1,0:T(1,128)} %copy.33), calls=%async_computation.4 | async-start | bytes 32768 | tf_op jit(solution)/shard_map/all_to_all | solution.py:117
  208.6 17.5 %all-to-all-start.6 = ((f32[16,32,128]{2,1,0:T(8,128)}), f32[16,32,128]{2,1,0:T(8,128)}, u32[]{:S(2)}, u32[]{:S(2)}) async-start(f32[16,32,128]{2,1,0:T(8,128)} %broadcast_in_dim.23), calls=%async_computation.6 | async-start | bytes 524288 | tf_op jit(solution)/shard_map/all_to_all | solution.py:165
  215.0 38.8 %collective-permute-start.4 = (f32[32,256]{1,0:T(8,128)}, f32[32,256]{1,0:T(8,128)}, u32[]{:S(2)}, u32[]{:S(2)}) collective-permute-start(f32[32,256]{1,0:T(8,128)} %pad_maximum_fusion.2), channel_id=1, source_target_pairs={{0,0},{1,1},{2,2},{3,3},{4,128},{5,129},{6,130},{7,131},{8,256},{9... | collective-permute-start | bytes 98312 | tf_op jit(solution)/shard_map/ppermute | solution.py:136
  226.2 7.7 %slice-start = ((s8[6291456]{0:T(1024)(128)(4,1)}), s8[2097152]{0:T(1024)(128)(4,1)S(1)}, s32[]{:S(2)}) async-start(s8[6291456]{0:T(1024)(128)(4,1)} %bitcast.77), calls=%async_computation.8 | async-start | bytes 4194304
  229.8 3.0 %copy-start.4 = (bf16[384,768]{1,0:T(8,128)(2,1)S(1)}, bf16[384,768]{1,0:T(8,128)(2,1)}, u32[]{:S(2)}) copy-start(bf16[384,768]{1,0:T(8,128)(2,1)} %copy-done.3) | copy-start | bytes 1769476
  229.8 3.5 %copy-start.10 = (f32[1,4096]{1,0:T(1,128)S(1)}, f32[1,4096]{1,0:T(1,128)}, u32[]{:S(2)}) copy-start(f32[1,4096]{1,0:T(1,128)} %get-tuple-element.5) | copy-start | bytes 49156
  229.9 4.0 %slice-start.1 = ((s8[6291456]{0:T(1024)(128)(4,1)}), s8[4194304]{0:T(1024)(128)(4,1)S(1)}, s32[]{:S(2)}) async-start(s8[6291456]{0:T(1024)(128)(4,1)} %bitcast.77), calls=%async_computation.9 | async-start | bytes 8388608
  238.7 15.1 %copy-start.11 = (f32[1,256]{1,0:T(1,128)S(1)}, f32[1,256]{1,0:T(1,128)}, u32[]{:S(2)}) copy-start(f32[1,256]{1,0:T(1,128)} %constant_dynamic-slice_fusion.1) | copy-start | bytes 3076
  238.7 27.8 %copy-start.13 = (s32[128]{0:T(128)S(1)}, s32[128]{0:T(128)}, u32[]{:S(2)}) copy-start(s32[128]{0:T(128)} %copy-done.12) | copy-start | bytes 1540
  240.6 25.8 %all-to-all-start.5 = ((bf16[32,12,512]{2,1,0:T(8,128)(2,1)}), bf16[32,12,512]{2,1,0:T(8,128)(2,1)S(1)}, u32[]{:S(2)}, u32[]{:S(2)}) async-start(bf16[32,12,512]{2,1,0:T(8,128)(2,1)} %reshape.187), calls=%async_computation.5 | async-start | bytes 1048576 | tf_op jit(solution)/shard_map/all_to_all | solution.py:154
Sparse Core Ops, SparseCore 0:
  10.0 56.2 all-gather.1
